TPU v7x, 32 devices: a whole 2x2x4 slice. The times are simulated.
32 devices in a mesh: group: 8 (over z, x), local: 4 (over y, core).
Axes of the slice: x: 2, y: 2, z: 4, core: 2. Of those that a mesh axis runs over, the one named last changes fastest.
Arguments:
- tokens: bfloat16 [256, 3584], P(('group', 'local')), may hold values from -6 to 6
- routes: int32 [256, 8], P(('group', 'local')), may hold values from 0 to 31, as said below
- route_gates: float32 [256, 8], P(('group', 'local')), may hold values from 0.2 to 2
- gate_weight: bfloat16 [32, 3584, 1024], P(('group', 'local')), may hold values from -0.09375 to 0.09375
- up_weight: bfloat16 [32, 3584, 1024], P(('group', 'local')), may hold values from -0.09375 to 0.09375
Outputs:
- routed_hidden: bfloat16 [32, 128, 1024], P(('group', 'local'))
Inputs may be any that keep to these rules, and one draw needn't show every extreme that they name: `routes`: each token names 8 different experts, lying in exactly 4 of the 8 expert groups of 4 consecutive experts; in each aligned block of 2 tokens every block of 4 consecutive experts is used by exactly one token, which names 2 of its experts.
All inputs are finite; a program needn't handle non-finite values.
Results may differ from a plain program's by a relative error of at most 0.012.
Values may be sent and summed in bfloat16 or wider, within the bound.
A program may use at most 64 MiB of HBM per device.

v0:
```python
import jax
import jax.numpy as jnp
from jax import lax
from jax.sharding import PartitionSpec as P

NEG = 8
EXP_MESH = 4
TOPG = 4
TOP = 8


def over_all(x, axis, dim, block):
    whole = lax.all_gather(x, axis, axis=dim, tiled=True)
    return block(whole, jnp.int32(0))


def pack_rows(tokens, routes, route_gates, n_group):
    quarters = n_group // NEG
    per_token = TOPG * min(TOP // TOPG, quarters)
    per_group = tokens.shape[0] * per_token // n_group
    group_range = jnp.arange(n_group, dtype=jnp.int32)
    member = jnp.any((routes // EXP_MESH)[:, :, None] == group_range[None, None, :], axis=1).astype(
        jnp.int32
    )
    position = jnp.cumsum(member, axis=0) - 1
    slot_range = jnp.arange(per_group, dtype=jnp.int32)
    chosen = (member.T[:, None, :] == 1) & (position.T[:, None, :] == slot_range[None, :, None])
    packed = jnp.einsum(
        "gjt,td->gjd", chosen.astype(jnp.bfloat16), tokens, preferred_element_type=jnp.float32
    ).astype(jnp.bfloat16)
    expert_grid = group_range[:, None] * EXP_MESH + jnp.arange(EXP_MESH, dtype=jnp.int32)[None, :]
    matches = (routes[:, :, None, None] == expert_grid[None, None, :, :]).astype(jnp.float32)
    dense_gates = jnp.sum(route_gates[:, :, None, None] * matches, axis=1)
    packed_gates = jnp.einsum(
        "gjt,tgs->gjs", chosen.astype(jnp.float32), dense_gates, precision=lax.Precision.HIGHEST
    )
    return (packed, packed_gates)


def expand(token_rows, row_gates, gate_weight, up_weight, slot_index):
    lead_shape = token_rows.shape[:-1]
    flat_rows = token_rows.reshape(-1, token_rows.shape[-1])
    picker = (jnp.arange(row_gates.shape[-1], dtype=jnp.int32) == slot_index).astype(jnp.float32)
    scaling = jnp.sum(row_gates * picker, axis=-1).reshape(-1, 1)
    pre_gate = jnp.dot(flat_rows, gate_weight[0], preferred_element_type=jnp.float32)
    pre_up = jnp.dot(flat_rows, up_weight[0], preferred_element_type=jnp.float32)
    hidden = (jax.nn.silu(pre_gate) * pre_up * scaling).astype(jnp.bfloat16)
    return hidden.reshape(lead_shape + (hidden.shape[-1],))


def shards(tokens, routes, route_gates, gate_weight, up_weight):
    n_group = lax.axis_size("group")
    slot_index = lax.axis_index("local") // (lax.axis_size("local") // EXP_MESH)
    packed, packed_gates = pack_rows(tokens, routes, route_gates, n_group)

    def compute_pieces(pieces_in):
        return expand(pieces_in[0], pieces_in[1], gate_weight, up_weight, slot_index)

    received = (
        lax.all_to_all(packed, "group", split_axis=0, concat_axis=0, tiled=True),
        lax.all_to_all(
            packed_gates.astype(jnp.bfloat16), "group", split_axis=0, concat_axis=0, tiled=True
        ).astype(packed_gates.dtype),
    )
    result = over_all(
        (received[0], received[1].astype(jnp.bfloat16)),
        "local",
        1,
        lambda piece, start: compute_pieces((piece[0], piece[1].astype(jnp.float32))),
    )
    return result.reshape(1, -1, result.shape[-1])


def solution(mesh):
    placed = (
        P(("group", "local"), None),
        P(("group", "local"), None),
        P(("group", "local"), None),
        P(("group", "local"), None, None),
        P(("group", "local"), None, None),
    )
    return jax.shard_map(
        shards,
        mesh=mesh,
        in_specs=placed,
        out_specs=P(("group", "local"), None, None),
        check_vma=False,
    )
```

profile of v0, /device:TPU:0, one launch (start us, length us, event | category | flops | bytes accessed | tf_op | source)
XLA Modules:
  0.0 44.4 jit_solution(3490072577197885858)
XLA Ops:
  0.0 0.0 copy-start
  0.0 0.7 %add_select_fusion = s32[8,8]{1,0:T(8,128)S(1)} fusion(s32[8,8]{1,0:T(8,128)} %param.6), kind=kLoop, calls=%fused_computation.18 | loop fusion | flops 960 | bytes 512 | tf_op jit(solution)/shard_map/jit(floor_divide)/jit(_where)/select_n | solution.py:22
  0.7 0.1 fusion.17
  0.8 0.1 copy.28
  0.9 0.1 copy.29
  1.0 0.8 %select_reduce_fusion = f32[8,8,4]{1,2,0:T(4,128)S(1)} fusion(f32[8,8]{1,0:T(8,128)} %param.7, s32[8,4]{0,1:T(4,128)S(1)} %iota_add_fusion, s32[8,8]{1,0:T(8,128)} %param.6), kind=kLoop, calls=%fused_computation.10 | loop fusion | flops 5888 | bytes 1664 | tf_op jit(solution)/shard_map/reduce_sum | solution.py:33
  1.9 0.1 copy.34
  2.0 0.8 %convolution_convert_fusion.1 = bf16[8,4,4]{2,1,0:T(4,128)(2,1)} fusion(pred[8,4,8]{2,1,0:T(4,128)(4,1)S(1)} %fusion.18, f32[8,8,4]{0,2,1:T(4,128)S(1)} %copy.34), kind=kOutput, calls=%fused_computation.9 | convolution fusion | flops 12416 | bytes 1536 | tf_op jit(solution)/shard_map/gjt,tgs->gjs/dot_general | solution.py:34
  2.7 7.3 %all-to-all-start.1 = ((bf16[8,4,4]{2,1,0:T(4,128)(2,1)}), bf16[8,4,4]{2,1,0:T(4,128)(2,1)S(1)}, u32[]{:S(2)}, u32[]{:S(2)}) async-start(bf16[8,4,4]{2,1,0:T(4,128)(2,1)} %convolution_convert_fusion.1), calls=%async_computation.1 | async-start | bytes 16384 | tf_op jit(solution)/shard_map/all_to_all | solution.py:61
  10.0 0.0 copy-done
  10.0 0.2 convolution_convert_fusion
  10.2 0.8 %copy.31 = bf16[8,4,3584]{2,1,0:T(4,128)(2,1)} copy(bf16[8,4,3584]{2,0,1:T(8,128)(2,1)S(1)} %convolution_convert_fusion) | data formatting | bytes 458752 | tf_op jit(solution)/shard_map/convert_element_type | solution.py:30
  11.0 5.5 %all-to-all-done.1 = bf16[8,4,4]{2,1,0:T(4,128)(2,1)S(1)} async-done(((bf16[8,4,4]{2,1,0:T(4,128)(2,1)}), bf16[8,4,4]{2,1,0:T(4,128)(2,1)S(1)}, u32[]{:S(2)}, u32[]{:S(2)}) %all-to-all-start.1) | async-done | bytes 288 | tf_op jit(solution)/shard_map/all_to_all | solution.py:61
  16.5 3.4 %all-to-all-start = ((bf16[8,4,3584]{2,1,0:T(4,128)(2,1)}), bf16[8,4,3584]{2,1,0:T(4,128)(2,1)S(1)}, u32[]{:S(2)}, u32[]{:S(2)}) async-start(bf16[8,4,3584]{2,1,0:T(4,128)(2,1)} %copy.31), calls=%async_computation | async-start | bytes 458752 | tf_op jit(solution)/shard_map/all_to_all | solution.py:60
  19.9 0.1 copy.35
  20.0 5.2 %all_gather.7 = bf16[8,16,4]{0,2,1:T(4,128)(2,1)S(1)} all-gather(bf16[8,4,4]{0,2,1:T(4,128)(2,1)S(1)} %copy.35), channel_id=1, replica_groups=mesh['group'=8,'local'=4] {'local'}, dimensions={1}, use_global_device_ids=true | all-gather | bytes 1280 | tf_op jit(solution)/shard_map/all_gather | solution.py:13
  25.2 0.1 multiply_reduce_fusion
  25.3 0.1 copy.36
  25.4 0.1 mul.48
  25.4 2.4 %all-to-all-done = bf16[8,4,3584]{2,1,0:T(4,128)(2,1)S(1)} async-done(((bf16[8,4,3584]{2,1,0:T(4,128)(2,1)}), bf16[8,4,3584]{2,1,0:T(4,128)(2,1)S(1)}, u32[]{:S(2)}, u32[]{:S(2)}) %all-to-all-start) | async-done | bytes 229408 | tf_op jit(solution)/shard_map/all_to_all | solution.py:60
  27.9 9.3 %all_gather.6 = bf16[8,16,3584]{2,0,1:T(8,128)(2,1)S(1)} all-gather(bf16[8,4,3584]{2,0,1:T(8,128)(2,1)S(1)} %copy.32), channel_id=1, replica_groups=mesh['group'=8,'local'=4] {'local'}, dimensions={1}, use_global_device_ids=true | all-gather | bytes 1146880 | tf_op jit(solution)/shard_map/all_gather | solution.py:13
  37.2 0.0 slice-start
  37.2 0.3 copy.33
  37.5 0.0 slice-start.1
  37.5 4.3 %fusion.2 = f32[128,1024]{1,0:T(8,128)S(1)} fusion(bf16[128,3584]{1,0:T(8,128)(2,1)S(1)} %bitcast.28, bf16[1,3584,1024]{2,1,0:T(8,128)(2,1)} %param.8), kind=kOutput, calls=%fused_computation.2 | convolution fusion | flops 939524096 | bytes 8781824 | tf_op jit(solution)/shard_map/dot_general | solution.py:45
  41.9 0.0 slice-done
  41.9 0.7 %slice-done.1 = s8[3145728]{0:T(1024)(128)(4,1)S(1)} async-done(((s8[7340032]{0:T(1024)(128)(4,1)}), s8[3145728]{0:T(1024)(128)(4,1)S(1)}, s32[]{:S(2)}) %slice-start.1) | async-done | bytes 3145752
  42.5 1.9 %fusion.13 = bf16[1,128,1024]{2,1,0:T(8,128)(2,1)} fusion(bf16[128,3584]{1,0:T(8,128)(2,1)S(1)} %bitcast.29, bf16[1,3584,1024]{2,1,0:T(8,128)(2,1)S(1)} %bitcast.31, f32[128,1024]{1,0:T(8,128)S(1)} %fusion.2, f32[128]{0:T(128)S(1)} %mul.48), kind=kOutput, calls=%fused_computation.8 | convolution fusion | flops 940441600 | bytes 9044480 | tf_op jit(solution)/shard_map/dot_general | solution.py:46
  (9 shorter events, 0.1 us)
Async XLA Ops:
  0.0 10.0 %copy-start = (bf16[8,3584]{1,0:T(8,128)(2,1)S(1)}, bf16[8,3584]{1,0:T(8,128)(2,1)}, u32[]{:S(2)}) copy-start(bf16[8,3584]{1,0:T(8,128)(2,1)} %param.5) | copy-start | bytes 172036
  2.7 13.8 %all-to-all-start.1 = ((bf16[8,4,4]{2,1,0:T(4,128)(2,1)}), bf16[8,4,4]{2,1,0:T(4,128)(2,1)S(1)}, u32[]{:S(2)}, u32[]{:S(2)}) async-start(bf16[8,4,4]{2,1,0:T(4,128)(2,1)} %convolution_convert_fusion.1), calls=%async_computation.1 | async-start | bytes 16384 | tf_op jit(solution)/shard_map/all_to_all | solution.py:61
  16.5 11.3 %all-to-all-start = ((bf16[8,4,3584]{2,1,0:T(4,128)(2,1)}), bf16[8,4,3584]{2,1,0:T(4,128)(2,1)S(1)}, u32[]{:S(2)}, u32[]{:S(2)}) async-start(bf16[8,4,3584]{2,1,0:T(4,128)(2,1)} %copy.31), calls=%async_computation | async-start | bytes 458752 | tf_op jit(solution)/shard_map/all_to_all | solution.py:60
  37.2 4.6 %slice-start = ((s8[7340032]{0:T(1024)(128)(4,1)}), s8[4194304]{0:T(1024)(128)(4,1)S(1)}, s32[]{:S(2)}) async-start(s8[7340032]{0:T(1024)(128)(4,1)} %bitcast.30), calls=%async_computation.2 | async-start | bytes 8388608
  37.5 5.1 %slice-start.1 = ((s8[7340032]{0:T(1024)(128)(4,1)}), s8[3145728]{0:T(1024)(128)(4,1)S(1)}, s32[]{:S(2)}) async-start(s8[7340032]{0:T(1024)(128)(4,1)} %bitcast.30), calls=%async_computation.3 | async-start | bytes 6291456
where the time goes:
time: 44.8 us; the launch traced here: 44.4 us
  blocking collectives  14.5 us (32%)
  starting transfers between devices  10.7 us (24%)
  waiting for transfers between devices  7.89 us (18%)
  matrix products  7.19 us (16%)
  local copies, waits for them, and re-layouts  2.31 us (5%)
  other arithmetic  1.79 us (4%)
    all_gather x2, blocking collectives, over_all(): whole = lax.all_gather(x, axis, axis=dim, tiled=True)  14.5 us
    all_to_all x1, starting transfers between devices, shards(): lax.all_to_all(packed_gates.astype(jnp.bfloat16), 'group', split_axis=0,...  7.25 us
    all_to_all x1, waiting for transfers between devices, shards(): lax.all_to_all(packed_gates.astype(jnp.bfloat16), 'group', split_axis=0,...  5.51 us
    dot_general x1, matrix products, expand(): jnp.dot(flat_rows, gate_weight[0], preferred_element_type=jnp.float32)  4.35 us
    all_to_all x1, starting transfers between devices, shards(): lax.all_to_all(packed, 'group', split_axis=0, concat_axis=0, tiled=True)  3.4 us
    all_to_all x1, waiting for transfers between devices, shards(): lax.all_to_all(packed, 'group', split_axis=0, concat_axis=0, tiled=True)  2.39 us
    dot_general x1, matrix products, expand(): jnp.dot(flat_rows, up_weight[0], preferred_element_type=jnp.float32)  1.9 us
  transfers between devices with their start and end apart: 2, of which 2 were waited for; matrix products, arithmetic and copies ran while one was open for 3% of the time, Pallas kernels for 0%

commit v1 on v0

v1 whole, which is shorter than its diff:
```python
import functools

import jax
import jax.numpy as jnp
from jax import lax
from jax.experimental import pallas as pl
from jax.experimental.pallas import tpu as pltpu
from jax.sharding import PartitionSpec as P

NEG = 8
EXP_MESH = 4
TOPG = 4
TOP = 8
LANES = 128
ROW_TILE = 16
CORES = 2


def block_tokens(n_group):
    return n_group // (TOPG * min(TOP // TOPG, n_group // NEG))


def kernel(
    n_group,
    n_local,
    tok_ref,
    rt_ref,
    ga_ref,
    gw_hbm,
    uw_hbm,
    out_ref,
    stage,
    recv_a,
    send_b,
    x0,
    x1,
    x2,
    x3,
    wg,
    wu,
    acc_g,
    acc_u,
    w_sem,
    a_send,
    a_recv,
    b_send,
    b_recv,
    c_send,
    x1_recv,
    x2_recv,
    x3_recv,
):
    g = lax.axis_index("group")
    me = lax.axis_index("local")
    n_tok, depth = tok_ref.shape
    chunk = depth // n_local
    block = block_tokens(n_group)
    piece = n_local * n_tok // block
    rows = n_group * piece
    n_top = rt_ref.shape[1]

    core = lax.rem(me, CORES)
    l_core = me + 1 - 2 * core
    l_y = lax.rem(me + CORES, n_local)
    l_diag = lax.rem(l_core + CORES, n_local)

    barrier = pltpu.get_barrier_semaphore()
    for k in range(1, n_local):
        pl.semaphore_signal(
            barrier, inc=1, device_id={"local": lax.rem(me + k, n_local)}, device_id_type=pl.DeviceIdType.MESH
        )
    for k in range(1, n_group):
        pl.semaphore_signal(
            barrier, inc=1, device_id={"group": lax.rem(g + k, n_group)}, device_id_type=pl.DeviceIdType.MESH
        )

    loads = []
    for slot, part in enumerate((me, l_core, l_y, l_diag)):
        at = pl.ds(pl.multiple_of(part * chunk, LANES), chunk)
        for i, (src, dst) in enumerate(((gw_hbm, wg), (uw_hbm, wu))):
            load = pltpu.make_async_copy(src.at[0, at, :], dst.at[slot], w_sem.at[slot, i])
            load.start()
            loads.append(load)

    lane = lax.broadcasted_iota(jnp.int32, (n_tok, LANES), 1)
    m = lax.broadcasted_iota(jnp.int32, (n_tok, rows), 1)
    t = lax.broadcasted_iota(jnp.int32, (n_tok, rows), 0) + me * n_tok
    routes = rt_ref[...]
    gates = ga_ref[...]
    dense = jnp.zeros((n_tok, LANES), jnp.float32)
    member = jnp.zeros((n_tok, rows), jnp.float32)
    for k in range(n_top):
        r = routes[:, k : k + 1]
        dense = dense + jnp.where(lane == r, gates[:, k : k + 1], 0.0)
        member = jnp.where((r >= (m // piece) * EXP_MESH) & (r < (m // piece + 1) * EXP_MESH), 1.0, member)
    chosen = jnp.where(t // block == lax.rem(m, piece), member, 0.0)
    for j in range(n_local):
        stage[j, :, :chunk] = tok_ref[:, j * chunk : (j + 1) * chunk]
        stage[j, :, chunk : chunk + LANES] = dense.astype(jnp.bfloat16)
        stage[j, :, chunk + LANES :] = chosen.astype(jnp.bfloat16)
    recv_a[me] = stage[me]

    pl.semaphore_wait(barrier, n_local - 1 + n_group - 1)

    sends = []
    for k in range(1, n_local):
        to = lax.rem(me + k, n_local)
        copy = pltpu.make_async_remote_copy(
            src_ref=stage.at[to],
            dst_ref=recv_a.at[me],
            send_sem=a_send.at[k],
            recv_sem=a_recv.at[k],
            device_id={"local": to},
            device_id_type=pl.DeviceIdType.MESH,
        )
        copy.start()
        sends.append(copy)
    for copy in sends:
        copy.wait_recv()

    got = jnp.concatenate([recv_a[j].astype(jnp.float32) for j in range(n_local)], axis=0).astype(jnp.bfloat16)
    packed = lax.dot_general(
        got[:, chunk + LANES :],
        got[:, : chunk + LANES],
        (((0,), (0,)), ((), ())),
        preferred_element_type=jnp.float32,
    ).astype(jnp.bfloat16)
    send_b[...] = packed.reshape(n_group, piece, chunk + LANES)

    far_first = sorted(range(1, n_group), key=lambda k: -min(k, n_group - k))
    for k in far_first:
        to = lax.rem(g + k, n_group)
        copy = pltpu.make_async_remote_copy(
            src_ref=send_b.at[to],
            dst_ref=x0.at[g],
            send_sem=b_send.at[k],
            recv_sem=b_recv.at[k],
            device_id={"group": to},
            device_id_type=pl.DeviceIdType.MESH,
        )
        copy.start()
        sends.append(copy)
    x0[g] = send_b[g]

    def onward(src, dst, at, send, recv, to):
        copy = pltpu.make_async_remote_copy(
            src_ref=src,
            dst_ref=dst.at[at],
            send_sem=send,
            recv_sem=recv,
            device_id={"local": to},
            device_id_type=pl.DeviceIdType.MESH,
        )
        copy.start()
        sends.append(copy)
        return copy

    order = [0] + far_first[::-1]
    b_copy = dict(zip(far_first, sends[n_local - 1 :]))
    core_in, y_in, diag_in = [], [], []

    def forward(step):
        at = lax.rem(g + n_group - order[step], n_group)
        y_in[step].wait_recv()
        diag_in.append(onward(x2.at[at], x3, at, c_send.at[2, step], x3_recv.at[step], l_core))

    lag = 2
    for step, k in enumerate(order):
        if k:
            b_copy[k].wait_recv()
        at = lax.rem(g + n_group - k, n_group)
        src = x0.at[at, :, pl.ds(0, chunk)]
        y_in.append(onward(src, x2, at, c_send.at[1, step], x2_recv.at[step], l_y))
        core_in.append(onward(src, x1, at, c_send.at[0, step], x1_recv.at[step], l_core))
        if step >= lag:
            forward(step - lag)

    def rows_of(x):
        return x[:, :, :chunk].reshape(rows, chunk)

    def add(slot, x, first=False):
        for load in loads[2 * slot : 2 * slot + 2]:
            load.wait()
        a = rows_of(x)
        for w, acc in ((wg, acc_g), (wu, acc_u)):
            p = jnp.dot(a, w[slot], preferred_element_type=jnp.float32)
            acc[...] = p if first else acc[...] + p

    add(0, x0, True)
    for step in range(n_group - lag, n_group):
        forward(step)
    for copy in core_in:
        copy.wait_recv()
    add(1, x1)
    add(2, x2)
    for copy in diag_in:
        copy.wait_recv()
    for load in loads[6:8]:
        load.wait()

    expert = g * EXP_MESH + me // (n_local // EXP_MESH)
    gate_rows = x0[:, :, chunk:].reshape(rows, LANES).astype(jnp.float32)
    mine = lax.broadcasted_iota(jnp.int32, (rows, LANES), 1) == expert
    scale = jnp.sum(jnp.where(mine, gate_rows, 0.0), axis=1, keepdims=True)
    a = rows_of(x3)
    width = 256
    for n in range(0, out_ref.shape[2], width):
        at = slice(n, n + width)
        pg = acc_g[:, at] + jnp.dot(a, wg[3, :, at], preferred_element_type=jnp.float32)
        pu = acc_u[:, at] + jnp.dot(a, wu[3, :, at], preferred_element_type=jnp.float32)
        out_ref[0, :, at] = (pg / (1.0 + jnp.exp(-pg)) * pu * scale).astype(jnp.bfloat16)

    for copy in sends:
        copy.wait_send()


def fused(tokens, routes, route_gates, gate_weight, up_weight):
    n_group, n_local = lax.axis_size("group"), lax.axis_size("local")
    n_tok, depth = tokens.shape
    hidden = gate_weight.shape[-1]
    chunk = depth // n_local
    piece = n_local * n_tok // block_tokens(n_group)
    rows = n_group * piece
    bf16, f32 = jnp.bfloat16, jnp.float32
    vmem = pl.BlockSpec(memory_space=pltpu.VMEM)
    hbm = pl.BlockSpec(memory_space=pl.ANY)
    dma = pltpu.SemaphoreType.DMA
    return pl.pallas_call(
        functools.partial(kernel, n_group, n_local),
        out_shape=jax.ShapeDtypeStruct((1, rows, hidden), bf16),
        in_specs=[vmem, vmem, vmem, hbm, hbm],
        out_specs=vmem,
        scratch_shapes=[
            pltpu.VMEM((n_local, n_tok, chunk + LANES + rows), bf16),
            pltpu.VMEM((n_local, n_tok, chunk + LANES + rows), bf16),
            pltpu.VMEM((n_group, piece, chunk + LANES), bf16),
            pltpu.VMEM((n_group, piece, chunk + LANES), bf16),
            pltpu.VMEM((n_group, piece, chunk), bf16),
            pltpu.VMEM((n_group, piece, chunk), bf16),
            pltpu.VMEM((n_group, piece, chunk), bf16),
            pltpu.VMEM((n_local, chunk, hidden), bf16),
            pltpu.VMEM((n_local, chunk, hidden), bf16),
            pltpu.VMEM((rows, hidden), f32),
            pltpu.VMEM((rows, hidden), f32),
            dma((n_local, 2)),
            dma((n_local,)),
            dma((n_local,)),
            dma((n_group,)),
            dma((n_group,)),
            dma((3, n_group)),
            dma((n_group,)),
            dma((n_group,)),
            dma((n_group,)),
        ],
        compiler_params=pltpu.CompilerParams(
            collective_id=0, has_side_effects=True, vmem_limit_bytes=48 * 1024 * 1024
        ),
        cost_estimate=pl.CostEstimate(
            flops=4 * rows * depth * hidden,
            bytes_accessed=4 * depth * hidden + 2 * rows * hidden,
            transcendentals=rows * hidden,
        ),
    )(tokens, routes, route_gates, gate_weight, up_weight)


def staged(tokens, routes, route_gates, gate_weight, up_weight):
    n_group, n_local = lax.axis_size("group"), lax.axis_size("local")
    block = block_tokens(n_group)
    n_tok, depth = tokens.shape
    groups = jnp.arange(n_group, dtype=jnp.int32)
    member = jnp.any((routes // EXP_MESH)[:, :, None] == groups, axis=1).astype(jnp.bfloat16)
    packed = jnp.einsum(
        "ibg,ibd->gid",
        member.reshape(-1, block, n_group),
        tokens.reshape(-1, block, depth),
        preferred_element_type=jnp.float32,
    ).astype(jnp.bfloat16)
    experts = groups[:, None] * EXP_MESH + jnp.arange(EXP_MESH, dtype=jnp.int32)
    matches = (routes[:, :, None, None] == experts).astype(jnp.float32)
    dense = jnp.sum(route_gates[:, :, None, None] * matches, axis=1)
    gates = dense.reshape(-1, block, n_group, EXP_MESH).sum(axis=1).transpose(1, 0, 2).astype(jnp.bfloat16)

    def over(x):
        x = lax.all_to_all(x, "group", split_axis=0, concat_axis=0, tiled=True)
        x = lax.all_gather(x, "local", axis=1, tiled=True)
        return x.reshape(-1, x.shape[-1])

    x, scales = over(packed), over(gates).astype(jnp.float32)
    slot = lax.axis_index("local") // (n_local // EXP_MESH)
    mine = (jnp.arange(EXP_MESH, dtype=jnp.int32) == slot).astype(jnp.float32)
    scale = jnp.sum(scales * mine, axis=-1)[:, None]
    pre_gate = jnp.dot(x, gate_weight[0], preferred_element_type=jnp.float32)
    pre_up = jnp.dot(x, up_weight[0], preferred_element_type=jnp.float32)
    return (jax.nn.silu(pre_gate) * pre_up * scale).astype(jnp.bfloat16)[None]


def shards(tokens, routes, route_gates, gate_weight, up_weight):
    n_group, n_local = lax.axis_size("group"), lax.axis_size("local")
    piece = n_local * tokens.shape[0] // block_tokens(n_group)
    fits = (
        n_local == 2 * CORES
        and n_local % EXP_MESH == 0
        and tokens.shape[1] % (n_local * LANES) == 0
        and piece % ROW_TILE == 0
        and (n_group * piece) % LANES == 0
        and n_group * EXP_MESH <= LANES
        and gate_weight.shape[-1] % 256 == 0
    )
    plan = fused if fits else staged
    return plan(tokens, routes, route_gates, gate_weight, up_weight)


def solution(mesh):
    rows = P(("group", "local"), None)
    blocks = P(("group", "local"), None, None)
    return jax.shard_map(
        shards, mesh=mesh, in_specs=(rows, rows, rows, blocks, blocks), out_specs=blocks, check_vma=False
    )
```

time: 44.8 us -> 28.5 us (0.64)
  the two profiles are of different devices: /device:TPU:0 before, /device:TPU:15 now
where the time goes in v1:
time: 28.5 us; the launch traced here: 28.3 us
  Pallas kernels  25.4 us (89%)
  local copies, waits for them, and re-layouts  2.9 us (10%)
    pallas_call x1, Pallas kernels, fused(): pl.pallas_call(functools.partial(kernel, n_group, n_local), out_shape=jax...  25.4 us
    unnamed x7, local copies, waits for them, and re-layouts  2.9 us

profile of v1, /device:TPU:15, one launch (start us, length us, event | category | flops | bytes accessed | tf_op | source)
XLA Modules:
  0.0 28.3 jit_solution(4258211704954590418)
XLA Ops:
  0.0 0.0 copy-start
  0.0 0.8 %copy-done = bf16[8,3584]{1,0:T(8,128)(2,1)S(1)} copy-done((bf16[8,3584]{1,0:T(8,128)(2,1)S(1)}, bf16[8,3584]{1,0:T(8,128)(2,1)}, u32[]{:S(2)}) %copy-start) | copy-done | bytes 57368
  0.8 0.0 copy-start.1
  0.8 0.7 %copy-done.1 = s32[8,8]{1,0:T(8,128)S(1)} copy-done((s32[8,8]{1,0:T(8,128)S(1)}, s32[8,8]{1,0:T(8,128)}, u32[]{:S(2)}) %copy-start.1) | copy-done | bytes 280
  1.5 0.0 copy-start.2
  1.5 0.7 %copy-done.2 = f32[8,8]{1,0:T(8,128)S(1)} copy-done((f32[8,8]{1,0:T(8,128)S(1)}, f32[8,8]{1,0:T(8,128)}, u32[]{:S(2)}) %copy-start.2) | copy-done | bytes 280
  2.2 25.4 %shard_map.55 = bf16[1,128,1024]{2,1,0:T(8,128)(2,1)S(1)} custom-call(bf16[8,3584]{1,0:T(8,128)(2,1)S(1)} %copy-done, s32[8,8]{1,0:T(8,128)S(1)} %copy-done.1, f32[8,8]{1,0:T(8,128)S(1)} %copy-done.2, bf16[1,3584,1024]{2,1,0:T(8,128)(2,1)} %gw_hbm.1, bf16[1,3584,1024]{2,1,0:T(8,128)(2,1)} %uw_hbm.1), custom_call_target="tpu_custom_call" | custom-call | flops 1879048192 | bytes 14942208 | tf_op jit(solution)/shard_map/pallas_call | solution.py:228
  27.6 0.7 %copy.7 = bf16[1,128,1024]{2,1,0:T(8,128)(2,1)} copy(bf16[1,128,1024]{2,1,0:T(8,128)(2,1)S(1)} %shard_map.55) | data formatting | bytes 524288
Async XLA Ops:
  0.0 0.8 %copy-start = (bf16[8,3584]{1,0:T(8,128)(2,1)S(1)}, bf16[8,3584]{1,0:T(8,128)(2,1)}, u32[]{:S(2)}) copy-start(bf16[8,3584]{1,0:T(8,128)(2,1)} %tok_ref.1) | copy-start | bytes 172036
  0.8 0.7 %copy-start.1 = (s32[8,8]{1,0:T(8,128)S(1)}, s32[8,8]{1,0:T(8,128)}, u32[]{:S(2)}) copy-start(s32[8,8]{1,0:T(8,128)} %rt_ref.1) | copy-start | bytes 772
  1.5 0.7 %copy-start.2 = (f32[8,8]{1,0:T(8,128)S(1)}, f32[8,8]{1,0:T(8,128)}, u32[]{:S(2)}) copy-start(f32[8,8]{1,0:T(8,128)} %ga_ref.1) | copy-start | bytes 772

commit v2 on v1

--- a/solution.py
+++ b/solution.py
@@ -20,15 +20,27 @@
     return n_group // (TOPG * min(TOP // TOPG, n_group // NEG))
 
 
+def flip(index, bits):
+    bit = 1
+    while bit <= bits:
+        if bits & bit:
+            index = index + bit * (1 - 2 * lax.rem(index // bit, 2))
+        bit *= 2
+    return index
+
+
 def kernel(
     n_group,
     n_local,
+    tok_hbm,
+    rt_hbm,
+    ga_hbm,
+    gw_hbm,
+    uw_hbm,
+    out_ref,
     tok_ref,
     rt_ref,
     ga_ref,
-    gw_hbm,
-    uw_hbm,
-    out_ref,
     stage,
     recv_a,
     send_b,
@@ -40,6 +52,7 @@
     wu,
     acc_g,
     acc_u,
+    in_sem,
     w_sem,
     a_send,
     a_recv,
@@ -64,6 +77,11 @@
     l_y = lax.rem(me + CORES, n_local)
     l_diag = lax.rem(l_core + CORES, n_local)
 
+    small = []
+    for i, (src, dst) in enumerate(((tok_hbm, tok_ref), (rt_hbm, rt_ref), (ga_hbm, ga_ref))):
+        small.append(pltpu.make_async_copy(src, dst, in_sem.at[i]))
+        small[-1].start()
+
     barrier = pltpu.get_barrier_semaphore()
     for k in range(1, n_local):
         pl.semaphore_signal(
@@ -71,7 +89,7 @@
         )
     for k in range(1, n_group):
         pl.semaphore_signal(
-            barrier, inc=1, device_id={"group": lax.rem(g + k, n_group)}, device_id_type=pl.DeviceIdType.MESH
+            barrier, inc=1, device_id={"group": flip(g, k)}, device_id_type=pl.DeviceIdType.MESH
         )
 
     loads = []
@@ -82,6 +100,8 @@
             load.start()
             loads.append(load)
 
+    for copy in small:
+        copy.wait()
     lane = lax.broadcasted_iota(jnp.int32, (n_tok, LANES), 1)
     m = lax.broadcasted_iota(jnp.int32, (n_tok, rows), 1)
     t = lax.broadcasted_iota(jnp.int32, (n_tok, rows), 0) + me * n_tok
@@ -127,9 +147,9 @@
     ).astype(jnp.bfloat16)
     send_b[...] = packed.reshape(n_group, piece, chunk + LANES)
 
-    far_first = sorted(range(1, n_group), key=lambda k: -min(k, n_group - k))
-    for k in far_first:
-        to = lax.rem(g + k, n_group)
+    partners = range(1, n_group)
+    for k in partners:
+        to = flip(g, k)
         copy = pltpu.make_async_remote_copy(
             src_ref=send_b.at[to],
             dst_ref=x0.at[g],
@@ -155,20 +175,20 @@
         sends.append(copy)
         return copy
 
-    order = [0] + far_first[::-1]
-    b_copy = dict(zip(far_first, sends[n_local - 1 :]))
+    order = range(n_group)
+    b_copy = dict(zip(partners, sends[n_local - 1 :]))
     core_in, y_in, diag_in = [], [], []
 
     def forward(step):
-        at = lax.rem(g + n_group - order[step], n_group)
+        at = flip(g, order[step])
         y_in[step].wait_recv()
         diag_in.append(onward(x2.at[at], x3, at, c_send.at[2, step], x3_recv.at[step], l_core))
 
-    lag = 2
+    lag = 6
     for step, k in enumerate(order):
         if k:
             b_copy[k].wait_recv()
-        at = lax.rem(g + n_group - k, n_group)
+        at = flip(g, k)
         src = x0.at[at, :, pl.ds(0, chunk)]
         y_in.append(onward(src, x2, at, c_send.at[1, step], x2_recv.at[step], l_y))
         core_in.append(onward(src, x1, at, c_send.at[0, step], x1_recv.at[step], l_core))
@@ -228,9 +248,12 @@
     return pl.pallas_call(
         functools.partial(kernel, n_group, n_local),
         out_shape=jax.ShapeDtypeStruct((1, rows, hidden), bf16),
-        in_specs=[vmem, vmem, vmem, hbm, hbm],
+        in_specs=[hbm] * 5,
         out_specs=vmem,
         scratch_shapes=[
+            pltpu.VMEM(tokens.shape, tokens.dtype),
+            pltpu.VMEM(routes.shape, routes.dtype),
+            pltpu.VMEM(route_gates.shape, route_gates.dtype),
             pltpu.VMEM((n_local, n_tok, chunk + LANES + rows), bf16),
             pltpu.VMEM((n_local, n_tok, chunk + LANES + rows), bf16),
             pltpu.VMEM((n_group, piece, chunk + LANES), bf16),
@@ -242,6 +265,7 @@
             pltpu.VMEM((n_local, chunk, hidden), bf16),
             pltpu.VMEM((rows, hidden), f32),
             pltpu.VMEM((rows, hidden), f32),
+            dma((3,)),
             dma((n_local, 2)),
             dma((n_local,)),
             dma((n_local,)),
@@ -299,6 +323,7 @@
     piece = n_local * tokens.shape[0] // block_tokens(n_group)
     fits = (
         n_local == 2 * CORES
+        and n_group & (n_group - 1) == 0
         and n_local % EXP_MESH == 0
         and tokens.shape[1] % (n_local * LANES) == 0
         and piece % ROW_TILE == 0

time: 28.5 us -> 24.6 us (0.86)
  the two profiles are of different devices: /device:TPU:15 before, /device:TPU:0 now
where the time goes in v2:
time: 24.6 us; the launch traced here: 24.4 us
  Pallas kernels  21.5 us (87%)
  local copies, waits for them, and re-layouts  2.9 us (12%)
    pallas_call x1, Pallas kernels, fused(): pl.pallas_call(functools.partial(kernel, n_group, n_local), out_shape=jax...  21.5 us
    unnamed x7, local copies, waits for them, and re-layouts  2.9 us

profile of v2, /device:TPU:0, one launch (start us, length us, event | category | flops | bytes accessed | tf_op | source)
XLA Modules:
  0.0 24.4 jit_solution(10653139632237792005)
XLA Ops:
  0.0 0.0 copy-start
  0.0 0.8 %copy-done = bf16[8,3584]{1,0:T(8,128)(2,1)S(1)} copy-done((bf16[8,3584]{1,0:T(8,128)(2,1)S(1)}, bf16[8,3584]{1,0:T(8,128)(2,1)}, u32[]{:S(2)}) %copy-start) | copy-done | bytes 57368
  0.8 0.0 copy-start.1
  0.8 0.7 %copy-done.1 = s32[8,8]{1,0:T(8,128)S(1)} copy-done((s32[8,8]{1,0:T(8,128)S(1)}, s32[8,8]{1,0:T(8,128)}, u32[]{:S(2)}) %copy-start.1) | copy-done | bytes 280
  1.5 0.0 copy-start.2
  1.5 0.7 %copy-done.2 = f32[8,8]{1,0:T(8,128)S(1)} copy-done((f32[8,8]{1,0:T(8,128)S(1)}, f32[8,8]{1,0:T(8,128)}, u32[]{:S(2)}) %copy-start.2) | copy-done | bytes 280
  2.2 21.5 %shard_map.55 = bf16[1,128,1024]{2,1,0:T(8,128)(2,1)S(1)} custom-call(bf16[8,3584]{1,0:T(8,128)(2,1)S(1)} %copy-done, s32[8,8]{1,0:T(8,128)S(1)} %copy-done.1, f32[8,8]{1,0:T(8,128)S(1)} %copy-done.2, bf16[1,3584,1024]{2,1,0:T(8,128)(2,1)} %gw_hbm.1, bf16[1,3584,1024]{2,1,0:T(8,128)(2,1)} %uw_hbm.1), custom_call_target="tpu_custom_call" | custom-call | flops 1879048192 | bytes 14942208 | tf_op jit(solution)/shard_map/pallas_call | solution.py:248
  23.7 0.7 %copy.7 = bf16[1,128,1024]{2,1,0:T(8,128)(2,1)} copy(bf16[1,128,1024]{2,1,0:T(8,128)(2,1)S(1)} %shard_map.55) | data formatting | bytes 524288
Async XLA Ops:
  0.0 0.8 %copy-start = (bf16[8,3584]{1,0:T(8,128)(2,1)S(1)}, bf16[8,3584]{1,0:T(8,128)(2,1)}, u32[]{:S(2)}) copy-start(bf16[8,3584]{1,0:T(8,128)(2,1)} %tok_hbm.1) | copy-start | bytes 172036
  0.8 0.7 %copy-start.1 = (s32[8,8]{1,0:T(8,128)S(1)}, s32[8,8]{1,0:T(8,128)}, u32[]{:S(2)}) copy-start(s32[8,8]{1,0:T(8,128)} %rt_hbm.1) | copy-start | bytes 772
  1.5 0.7 %copy-start.2 = (f32[8,8]{1,0:T(8,128)S(1)}, f32[8,8]{1,0:T(8,128)}, u32[]{:S(2)}) copy-start(f32[8,8]{1,0:T(8,128)} %ga_hbm.1) | copy-start | bytes 772

commit v3 on v2

--- a/solution.py
+++ b/solution.py
@@ -62,6 +62,10 @@
     x1_recv,
     x2_recv,
     x3_recv,
+    v_out,
+    v_in,
+    v_send,
+    v_recv,
 ):
     g = lax.axis_index("group")
     me = lax.axis_index("local")
@@ -144,8 +148,8 @@
         got[:, : chunk + LANES],
         (((0,), (0,)), ((), ())),
         preferred_element_type=jnp.float32,
-    ).astype(jnp.bfloat16)
-    send_b[...] = packed.reshape(n_group, piece, chunk + LANES)
+    )
+    send_b[...] = packed[:, :chunk].astype(jnp.bfloat16).reshape(n_group, piece, chunk)
 
     partners = range(1, n_group)
     for k in partners:
@@ -162,6 +166,30 @@
         sends.append(copy)
     x0[g] = send_b[g]
 
+    row = lax.broadcasted_iota(jnp.int32, (rows, LANES), 0)
+    col = lax.broadcasted_iota(jnp.int32, (rows, LANES), 1)
+    slot = me // (n_local // EXP_MESH)
+    hers = jnp.where(col == (row // piece) * EXP_MESH + slot, packed[:, chunk:], 0.0)
+    hers = jnp.sum(hers, axis=1, keepdims=True)
+    place = lax.broadcasted_iota(jnp.int32, (rows, rows), 1)
+    from_row = lax.broadcasted_iota(jnp.int32, (rows, rows), 0)
+    spread = jnp.where(place == g * piece + lax.rem(from_row, piece), hers, 0.0)
+    v_out[...] = jnp.sum(spread.reshape(n_group, piece, rows), axis=1).reshape(n_group, 1, rows)
+    gate_in = []
+    for k in partners:
+        to = flip(g, k)
+        copy = pltpu.make_async_remote_copy(
+            src_ref=v_out.at[to],
+            dst_ref=v_in.at[g],
+            send_sem=v_send.at[k],
+            recv_sem=v_recv.at[k],
+            device_id={"group": to},
+            device_id_type=pl.DeviceIdType.MESH,
+        )
+        copy.start()
+        gate_in.append(copy)
+    v_in[g] = v_out[g]
+
     def onward(src, dst, at, send, recv, to):
         copy = pltpu.make_async_remote_copy(
             src_ref=src,
@@ -189,14 +217,14 @@
         if k:
             b_copy[k].wait_recv()
         at = flip(g, k)
-        src = x0.at[at, :, pl.ds(0, chunk)]
+        src = x0.at[at]
         y_in.append(onward(src, x2, at, c_send.at[1, step], x2_recv.at[step], l_y))
         core_in.append(onward(src, x1, at, c_send.at[0, step], x1_recv.at[step], l_core))
         if step >= lag:
             forward(step - lag)
 
     def rows_of(x):
-        return x[:, :, :chunk].reshape(rows, chunk)
+        return x[...].reshape(rows, chunk)
 
     def add(slot, x, first=False):
         for load in loads[2 * slot : 2 * slot + 2]:
@@ -218,10 +246,10 @@
     for load in loads[6:8]:
         load.wait()
 
-    expert = g * EXP_MESH + me // (n_local // EXP_MESH)
-    gate_rows = x0[:, :, chunk:].reshape(rows, LANES).astype(jnp.float32)
-    mine = lax.broadcasted_iota(jnp.int32, (rows, LANES), 1) == expert
-    scale = jnp.sum(jnp.where(mine, gate_rows, 0.0), axis=1, keepdims=True)
+    for copy in gate_in:
+        copy.wait_recv()
+    whole = jnp.sum(v_in[...].reshape(n_group, rows), axis=0, keepdims=True)
+    scale = jnp.sum(jnp.where(place == from_row, whole, 0.0), axis=1, keepdims=True)
     a = rows_of(x3)
     width = 256
     for n in range(0, out_ref.shape[2], width):
@@ -230,7 +258,7 @@
         pu = acc_u[:, at] + jnp.dot(a, wu[3, :, at], preferred_element_type=jnp.float32)
         out_ref[0, :, at] = (pg / (1.0 + jnp.exp(-pg)) * pu * scale).astype(jnp.bfloat16)
 
-    for copy in sends:
+    for copy in sends + gate_in:
         copy.wait_send()
 
 
@@ -256,8 +284,8 @@
             pltpu.VMEM(route_gates.shape, route_gates.dtype),
             pltpu.VMEM((n_local, n_tok, chunk + LANES + rows), bf16),
             pltpu.VMEM((n_local, n_tok, chunk + LANES + rows), bf16),
-            pltpu.VMEM((n_group, piece, chunk + LANES), bf16),
-            pltpu.VMEM((n_group, piece, chunk + LANES), bf16),
+            pltpu.VMEM((n_group, piece, chunk), bf16),
+            pltpu.VMEM((n_group, piece, chunk), bf16),
             pltpu.VMEM((n_group, piece, chunk), bf16),
             pltpu.VMEM((n_group, piece, chunk), bf16),
             pltpu.VMEM((n_group, piece, chunk), bf16),
@@ -273,6 +301,10 @@
             dma((n_group,)),
             dma((3, n_group)),
             dma((n_group,)),
+            dma((n_group,)),
+            dma((n_group,)),
+            pltpu.VMEM((n_group, 1, rows), f32),
+            pltpu.VMEM((n_group, 1, rows), f32),
             dma((n_group,)),
             dma((n_group,)),
         ],

time: 24.6 us -> 24.3 us (0.988)
  Pallas kernels: 21.5 us -> 21.1 us
    pallas_call x1, Pallas kernels: 21.5 us -> 21.1 us  [fused(): pl.pallas_call(functools.partial(kernel, n_group, n_local), out_shape=jax...]
where the time goes in v3:
time: 24.3 us; the launch traced here: 24 us
  Pallas kernels  21.1 us (87%)
  local copies, waits for them, and re-layouts  2.9 us (12%)
    pallas_call x1, Pallas kernels, fused(): pl.pallas_call(functools.partial(kernel, n_group, n_local), out_shape=jax...  21.1 us
    unnamed x7, local copies, waits for them, and re-layouts  2.9 us

profile of v3, /device:TPU:0, one launch (start us, length us, event | category | flops | bytes accessed | tf_op | source)
XLA Modules:
  0.0 24.0 jit_solution(15956101696844438496)
XLA Ops:
  0.0 0.0 copy-start
  0.0 0.8 %copy-done = bf16[8,3584]{1,0:T(8,128)(2,1)S(1)} copy-done((bf16[8,3584]{1,0:T(8,128)(2,1)S(1)}, bf16[8,3584]{1,0:T(8,128)(2,1)}, u32[]{:S(2)}) %copy-start) | copy-done | bytes 57368
  0.8 0.0 copy-start.1
  0.8 0.7 %copy-done.1 = s32[8,8]{1,0:T(8,128)S(1)} copy-done((s32[8,8]{1,0:T(8,128)S(1)}, s32[8,8]{1,0:T(8,128)}, u32[]{:S(2)}) %copy-start.1) | copy-done | bytes 280
  1.5 0.0 copy-start.2
  1.5 0.7 %copy-done.2 = f32[8,8]{1,0:T(8,128)S(1)} copy-done((f32[8,8]{1,0:T(8,128)S(1)}, f32[8,8]{1,0:T(8,128)}, u32[]{:S(2)}) %copy-start.2) | copy-done | bytes 280
  2.2 21.1 %shard_map.55 = bf16[1,128,1024]{2,1,0:T(8,128)(2,1)S(1)} custom-call(bf16[8,3584]{1,0:T(8,128)(2,1)S(1)} %copy-done, s32[8,8]{1,0:T(8,128)S(1)} %copy-done.1, f32[8,8]{1,0:T(8,128)S(1)} %copy-done.2, bf16[1,3584,1024]{2,1,0:T(8,128)(2,1)} %gw_hbm.1, bf16[1,3584,1024]{2,1,0:T(8,128)(2,1)} %uw_hbm.1), custom_call_target="tpu_custom_call" | custom-call | flops 1879048192 | bytes 14942208 | tf_op jit(solution)/shard_map/pallas_call | solution.py:276
  23.3 0.7 %copy.7 = bf16[1,128,1024]{2,1,0:T(8,128)(2,1)} copy(bf16[1,128,1024]{2,1,0:T(8,128)(2,1)S(1)} %shard_map.55) | data formatting | bytes 524288
Async XLA Ops:
  0.0 0.8 %copy-start = (bf16[8,3584]{1,0:T(8,128)(2,1)S(1)}, bf16[8,3584]{1,0:T(8,128)(2,1)}, u32[]{:S(2)}) copy-start(bf16[8,3584]{1,0:T(8,128)(2,1)} %tok_hbm.1) | copy-start | bytes 172036
  0.8 0.7 %copy-start.1 = (s32[8,8]{1,0:T(8,128)S(1)}, s32[8,8]{1,0:T(8,128)}, u32[]{:S(2)}) copy-start(s32[8,8]{1,0:T(8,128)} %rt_hbm.1) | copy-start | bytes 772
  1.5 0.7 %copy-start.2 = (f32[8,8]{1,0:T(8,128)S(1)}, f32[8,8]{1,0:T(8,128)}, u32[]{:S(2)}) copy-start(f32[8,8]{1,0:T(8,128)} %ga_hbm.1) | copy-start | bytes 772
